TPU v7x, 32 devices: a whole 2x2x4 slice. The times are simulated.
32 devices in a mesh: section: 4 (over y, x), expert: 8 (over z, core).
Axes of the slice: x: 2, y: 2, z: 4, core: 2. Of those that a mesh axis runs over, the one named last changes fastest.
Arguments:
- state: bfloat16 [2, 4, 512, 2048], P(None, 'section', 'expert'), may hold values from -6 to 6
- norm_gain: float32 [2, 4, 2048], P(None, 'section'), may hold values from 0.1 to 1.9
- up_weight: bfloat16 [2, 4, 8, 2048, 768], P(None, 'section', 'expert'), may hold values from -0.125 to 0.125
- down_weight: bfloat16 [2, 4, 8, 768, 2048], P(None, 'section', 'expert'), may hold values from -0.21875 to 0.21875
- expert_ids: int32 [4, 2, 4, 512, 2], P(None, None, 'section'), may hold values from 0 to 7, all different within a row; in each aligned block of 64 rows (0 to 63, 64 to 127, ..., all dimensions but the last counted through in order) at most 32 rows name the same one
- gate_values: float32 [4, 2, 4, 512, 2], P(None, None, 'section', 'expert'), may hold values from 0.1 to 1
Outputs:
- final_state: bfloat16 [2, 4, 512, 2048], P(None, 'section', 'expert')
- finished: bfloat16 [4, 512, 2048], P(None, 'expert', 'section')
Inputs may be any that keep to these rules, and one draw needn't show every extreme that they name: `expert_ids`: each token names two different experts. Within the 64 tokens of one index of expert (aligned blocks of 64 tokens) at one tick, slot and segment, no expert is named more than 32 times.
All inputs are finite; a program needn't handle non-finite values.
Results may differ from a plain program's by a relative error of at most 0.0095.
Values may be sent and summed in bfloat16 or wider, within the bound.
A program may use at most 64 MiB of HBM per device.

v0:
```python
import jax
import jax.numpy as jnp
from jax import lax
from jax.sharding import PartitionSpec as P


def from_behind(block, axis, distance):
    devices = range(lax.axis_size(axis))
    route = [((i - distance) % len(devices), i) for i in devices]
    return lax.ppermute(block, axis, route)


def spread(value, axis, root):
    mine = lax.axis_index(axis) == root
    return lax.psum(jnp.where(mine, value, jnp.zeros_like(value)), axis)


def rms_norm(layer_in, norm_gain):
    widened = layer_in.astype(jnp.float32)
    scaled = lax.rsqrt(jnp.mean(widened * widened, axis=-1, keepdims=True) + 1e-06)
    return (widened * scaled * norm_gain).astype(jnp.bfloat16)


def expert_mlp(in_rows, up_weight, down_weight):
    projected = jnp.einsum("srd,sdf->srf", in_rows, up_weight, preferred_element_type=jnp.float32)
    activated = jax.nn.silu(projected).astype(jnp.bfloat16)
    return jnp.einsum(
        "srf,sfd->srd", activated, down_weight, preferred_element_type=jnp.float32
    ).astype(jnp.bfloat16)


def source_bound(tok_rows, expert_count):
    return max(2, 4 * tok_rows // expert_count)


def through_exchange(layer_in, normed, up_weight, down_weight, routes, gates, expert_count, owner):
    slot_count, tok_rows, model_width = layer_in.shape
    per_source = source_bound(tok_rows, expert_count)
    own_routes = lax.dynamic_slice_in_dim(routes, owner * tok_rows, tok_rows, 1)
    matches = (own_routes[..., None] == jnp.arange(expert_count, dtype=jnp.int32)).astype(jnp.int32)
    flattened = matches.reshape(slot_count, tok_rows * 2, expert_count)
    earlier = (jnp.cumsum(flattened, axis=1) - flattened).reshape(
        slot_count, tok_rows, 2, expert_count
    )
    position = jnp.sum(earlier * matches, axis=3)
    slot_match = (position[..., None, None] == jnp.arange(per_source, dtype=jnp.int32)).astype(
        jnp.int32
    )
    chosen = matches[..., None] * slot_match
    dispatch = jnp.sum(chosen, axis=2).astype(jnp.bfloat16)
    weights = jnp.sum(chosen.astype(jnp.float32) * gates[..., None, None], axis=2)
    outgoing = jnp.einsum(
        "stjp,std->sjpd", dispatch, normed, preferred_element_type=jnp.float32
    ).astype(jnp.bfloat16)
    in_rows = lax.all_to_all(outgoing, "expert", split_axis=1, concat_axis=1, tiled=True)
    shaped = in_rows.reshape(slot_count, -1, model_width)
    outputs = expert_mlp(shaped, up_weight, down_weight).reshape(in_rows.shape)
    returned = lax.all_to_all(outputs, "expert", split_axis=1, concat_axis=1, tiled=True)
    combined = jnp.einsum(
        "stjp,sjpd->std", weights, returned.astype(jnp.float32), precision=lax.Precision.HIGHEST
    )
    return (layer_in.astype(jnp.float32) + combined).astype(jnp.bfloat16)


def advance(layer_in, norm_gain, up_weight, down_weight, routes, gates, expert_count, owner):
    normed = rms_norm(layer_in, norm_gain[:, None, :])
    return through_exchange(
        layer_in, normed, up_weight, down_weight, routes, gates, expert_count, owner
    )


def on_device(state, norm_gain, up_weight, down_weight, expert_ids, gate_values):
    expert_count = lax.axis_size("expert")
    segment_count = lax.axis_size("section")
    owner = lax.axis_index("expert")
    segment_place = lax.axis_index("section")
    gains = norm_gain[:, 0]
    up_local = up_weight[:, 0, 0]
    down_local = down_weight[:, 0, 0]
    current = state[:, 0]
    done_list = []
    for tick_index in range(expert_ids.shape[0]):
        routes = expert_ids[tick_index, :, 0]
        gates = gate_values[tick_index, :, 0]
        stepped = advance(current, gains, up_local, down_local, routes, gates, expert_count, owner)
        arrived = from_behind(stepped, "section", 1)
        at_start = segment_place == 0
        new_first = jnp.where(at_start, jnp.zeros_like(arrived[0]), arrived[0])
        new_second = jnp.where(at_start, arrived[0], arrived[1])
        done_list.append(arrived[1])
        current = jnp.stack([new_first, new_second])
    leaving = jnp.stack(done_list)
    leaving = spread(leaving, "section", 0)
    columns = leaving.shape[2] // segment_count
    finished = lax.dynamic_slice_in_dim(leaving, segment_place * columns, columns, 2)
    return (current[:, None], finished)


def solution(mesh):
    return jax.shard_map(
        on_device,
        mesh=mesh,
        in_specs=(
            P(None, "section", "expert", None),
            P(None, "section", None),
            P(None, "section", "expert", None, None),
            P(None, "section", "expert", None, None),
            P(None, None, "section", None, None),
            P(None, None, "section", "expert", None),
        ),
        out_specs=(P(None, "section", "expert", None), P(None, "expert", "section")),
        check_vma=False,
    )
```

profile of v0, /device:TPU:0, one launch (start us, length us, event | category | flops | bytes accessed | tf_op | source)
XLA Modules:
  0.0 612.4 jit_solution(907430167331132261)
XLA Ops:
  9.8 1.2 fusion.49
  12.1 55.2 %all_to_all.40 = bf16[2,8,32,2048]{3,2,0,1:T(8,128)(2,1)S(1)} all-to-all(bf16[2,8,32,2048]{3,2,0,1:T(8,128)(2,1)S(1)} %copy.61), channel_id=1, replica_groups=mesh['section'=4,'expert'=8] {'expert'}, dimensions={1} | all-to-all | bytes 4194304 | tf_op jit(solution)/shard_map/all_to_all | solution.py:55
  67.5 9.4 %fusion.16 = bf16[2,256,2048]{2,1,0:T(8,128)(2,1)} fusion(bf16[2,1,1,768,2048]{4,3,2,1,0:T(8,128)(2,1)} %param.9, bf16[2,256,2048]{2,1,0:T(8,128)(2,1)S(1)} %bitcast.151, bf16[2,1,1,2048,768]{4,3,2,1,0:T(8,128)(2,1)} %param.8), kind=kOutput, calls=%fused_computation.20 | convolution fusion | flops 3224240128 | bytes 16777216 | tf_op jit(solution)/shard_map/srf,sfd->srd/dot_general | solution.py:27
  76.9 3.1 copy.63
  80.0 3.7 all-to-all-start.1
  84.8 47.9 %all-to-all-done.1 = bf16[2,8,32,2048]{3,2,0,1:T(8,128)(2,1)S(1)} async-done(((bf16[2,8,32,2048]{3,2,0,1:T(8,128)(2,1)}), bf16[2,8,32,2048]{3,2,0,1:T(8,128)(2,1)S(1)}, u32[]{:S(2)}, u32[]{:S(2)}) %all-to-all-start.1) | async-done | bytes 2097184 | tf_op jit(solution)/shard_map/all_to_all | solution.py:58
  132.7 1.3 fusion.32
  134.0 1.5 collective-permute-start
  135.6 12.8 %collective-permute-done = bf16[2,64,2048]{2,1,0:T(8,128)(2,1)S(1)} collective-permute-done((bf16[2,64,2048]{2,1,0:T(8,128)(2,1)S(1)}, bf16[2,64,2048]{2,1,0:T(8,128)(2,1)S(1)}, u32[]{:S(2)}, u32[]{:S(2)}) %collective-permute-start) | collective-permute-done | bytes 524320 | tf_op jit(solution)/shard_map/ppermute | solution.py:10
  149.7 51.8 %all_to_all.41 = bf16[2,8,32,2048]{3,2,0,1:T(8,128)(2,1)S(1)} all-to-all(bf16[2,8,32,2048]{3,2,0,1:T(8,128)(2,1)S(1)} %copy.67), channel_id=1, replica_groups=mesh['section'=4,'expert'=8] {'expert'}, dimensions={1} | all-to-all | bytes 4194304 | tf_op jit(solution)/shard_map/all_to_all | solution.py:55
  201.6 9.4 %fusion.19 = bf16[2,256,2048]{2,1,0:T(8,128)(2,1)} fusion(bf16[2,1,1,768,2048]{4,3,2,1,0:T(8,128)(2,1)} %param.9, bf16[2,256,2048]{2,1,0:T(8,128)(2,1)S(1)} %bitcast.153, bf16[2,1,1,2048,768]{4,3,2,1,0:T(8,128)(2,1)} %param.8), kind=kOutput, calls=%fused_computation.21 | convolution fusion | flops 3224240128 | bytes 16777216 | tf_op jit(solution)/shard_map/srf,sfd->srd/dot_general | solution.py:27
  211.0 3.1 copy.69
  214.2 3.8 all-to-all-start.3
  219.1 47.6 %all-to-all-done.3 = bf16[2,8,32,2048]{3,2,0,1:T(8,128)(2,1)S(1)} async-done(((bf16[2,8,32,2048]{3,2,0,1:T(8,128)(2,1)}), bf16[2,8,32,2048]{3,2,0,1:T(8,128)(2,1)S(1)}, u32[]{:S(2)}, u32[]{:S(2)}) %all-to-all-start.3) | async-done | bytes 2097184 | tf_op jit(solution)/shard_map/all_to_all | solution.py:58
  266.8 1.3 fusion.33
  268.8 13.7 %collective-permute-done.1 = bf16[2,64,2048]{2,1,0:T(8,128)(2,1)S(1)} collective-permute-done((bf16[2,64,2048]{2,1,0:T(8,128)(2,1)S(1)}, bf16[2,64,2048]{2,1,0:T(8,128)(2,1)S(1)}, u32[]{:S(2)}, u32[]{:S(2)}) %collective-permute-start.1) | collective-permute-done | bytes 524320 | tf_op jit(solution)/shard_map/ppermute | solution.py:10
  283.7 51.8 %all_to_all.42 = bf16[2,8,32,2048]{3,2,0,1:T(8,128)(2,1)S(1)} all-to-all(bf16[2,8,32,2048]{3,2,0,1:T(8,128)(2,1)S(1)} %copy.73), channel_id=1, replica_groups=mesh['section'=4,'expert'=8] {'expert'}, dimensions={1} | all-to-all | bytes 4194304 | tf_op jit(solution)/shard_map/all_to_all | solution.py:55
  335.7 9.4 %fusion.22 = bf16[2,256,2048]{2,1,0:T(8,128)(2,1)} fusion(bf16[2,1,1,768,2048]{4,3,2,1,0:T(8,128)(2,1)} %param.9, bf16[2,256,2048]{2,1,0:T(8,128)(2,1)S(1)} %bitcast.155, bf16[2,1,1,2048,768]{4,3,2,1,0:T(8,128)(2,1)} %param.8), kind=kOutput, calls=%fused_computation.22 | convolution fusion | flops 3224240128 | bytes 16777216 | tf_op jit(solution)/shard_map/srf,sfd->srd/dot_general | solution.py:27
  345.1 3.1 copy.75
  348.2 3.6 all-to-all-start.5
  352.9 47.9 %all-to-all-done.5 = bf16[2,8,32,2048]{3,2,0,1:T(8,128)(2,1)S(1)} async-done(((bf16[2,8,32,2048]{3,2,0,1:T(8,128)(2,1)}), bf16[2,8,32,2048]{3,2,0,1:T(8,128)(2,1)S(1)}, u32[]{:S(2)}, u32[]{:S(2)}) %all-to-all-start.5) | async-done | bytes 2097184 | tf_op jit(solution)/shard_map/all_to_all | solution.py:58
  400.8 1.3 fusion.34
  402.2 14.3 %collective-permute-done.2 = bf16[2,64,2048]{2,1,0:T(8,128)(2,1)S(1)} collective-permute-done((bf16[2,64,2048]{2,1,0:T(8,128)(2,1)S(1)}, bf16[2,64,2048]{2,1,0:T(8,128)(2,1)S(1)}, u32[]{:S(2)}, u32[]{:S(2)}) %collective-permute-start.2) | collective-permute-done | bytes 524320 | tf_op jit(solution)/shard_map/ppermute | solution.py:10
  417.8 51.8 %all_to_all.43 = bf16[2,8,32,2048]{3,2,0,1:T(8,128)(2,1)S(1)} all-to-all(bf16[2,8,32,2048]{3,2,0,1:T(8,128)(2,1)S(1)} %copy.79), channel_id=1, replica_groups=mesh['section'=4,'expert'=8] {'expert'}, dimensions={1} | all-to-all | bytes 4194304 | tf_op jit(solution)/shard_map/all_to_all | solution.py:55
  469.7 9.4 %fusion.25 = bf16[2,256,2048]{2,1,0:T(8,128)(2,1)} fusion(bf16[2,1,1,768,2048]{4,3,2,1,0:T(8,128)(2,1)} %param.9, bf16[2,256,2048]{2,1,0:T(8,128)(2,1)S(1)} %bitcast.157, bf16[2,1,1,2048,768]{4,3,2,1,0:T(8,128)(2,1)} %param.8), kind=kOutput, calls=%fused_computation.23 | convolution fusion | flops 3224240128 | bytes 16777216 | tf_op jit(solution)/shard_map/srf,sfd->srd/dot_general | solution.py:27
  479.1 3.1 copy.81
  482.2 3.6 all-to-all-start.7
  486.7 48.1 %all-to-all-done.7 = bf16[2,8,32,2048]{3,2,0,1:T(8,128)(2,1)S(1)} async-done(((bf16[2,8,32,2048]{3,2,0,1:T(8,128)(2,1)}), bf16[2,8,32,2048]{3,2,0,1:T(8,128)(2,1)S(1)}, u32[]{:S(2)}, u32[]{:S(2)}) %all-to-all-start.7) | async-done | bytes 2097184 | tf_op jit(solution)/shard_map/all_to_all | solution.py:58
  534.8 2.2 fusion.35
  537.1 14.4 %collective-permute-done.3 = bf16[2,64,2048]{2,1,0:T(8,128)(2,1)S(1)} collective-permute-done((bf16[2,64,2048]{2,1,0:T(8,128)(2,1)S(1)}, bf16[2,64,2048]{2,1,0:T(8,128)(2,1)S(1)}, u32[]{:S(2)}, u32[]{:S(2)}) %collective-permute-start.3) | collective-permute-done | bytes 524320 | tf_op jit(solution)/shard_map/ppermute | solution.py:10
  553.6 50.3 %all-reduce.2.cloned.1.call-done = bf16[4,64,2048]{2,1,0:T(8,128)(2,1)} async-done(((bf16[4,64,2048]{2,1,0:T(8,128)(2,1)}), bf16[4,64,2048]{2,1,0:T(8,128)(2,1)}) %all-reduce.2.cloned.1.call-update) | async-done | bytes 1048592 | tf_op jit(solution)/shard_map/psum | solution.py:15
  603.8 1.7 constant_dynamic-slice_fusion.3
  (83 shorter events, 15.1 us)
Async XLA Ops:
  7.2 4.0 copy-start
  80.0 4.7 copy-start.1
  80.0 52.7 %all-to-all-start.1 = ((bf16[2,8,32,2048]{3,2,0,1:T(8,128)(2,1)}), bf16[2,8,32,2048]{3,2,0,1:T(8,128)(2,1)S(1)}, u32[]{:S(2)}, u32[]{:S(2)}) async-start(bf16[2,8,32,2048]{3,2,0,1:T(8,128)(2,1)} %copy.63), calls=%async_computation.1 | async-start | bytes 4194304 | tf_op jit(solution)/shard_map/all_to_all | solution.py:58
  134.0 14.4 %collective-permute-start = (bf16[2,64,2048]{2,1,0:T(8,128)(2,1)S(1)}, bf16[2,64,2048]{2,1,0:T(8,128)(2,1)S(1)}, u32[]{:S(2)}, u32[]{:S(2)}) collective-permute-start(bf16[2,64,2048]{2,1,0:T(8,128)(2,1)S(1)} %fusion.32), channel_id=1, source_target_pairs={{24,0},{0,8},{8,16},{16,24},{25,1},{1,9},{9,17},{17,25},{26,2},{2,... | collective-permute-start | bytes 1572872 | tf_op jit(solution)/shard_map/ppermute | solution.py:10
  214.2 52.6 %all-to-all-start.3 = ((bf16[2,8,32,2048]{3,2,0,1:T(8,128)(2,1)}), bf16[2,8,32,2048]{3,2,0,1:T(8,128)(2,1)S(1)}, u32[]{:S(2)}, u32[]{:S(2)}) async-start(bf16[2,8,32,2048]{3,2,0,1:T(8,128)(2,1)} %copy.69), calls=%async_computation.3 | async-start | bytes 4194304 | tf_op jit(solution)/shard_map/all_to_all | solution.py:58
  268.0 14.4 %collective-permute-start.1 = (bf16[2,64,2048]{2,1,0:T(8,128)(2,1)S(1)}, bf16[2,64,2048]{2,1,0:T(8,128)(2,1)S(1)}, u32[]{:S(2)}, u32[]{:S(2)}) collective-permute-start(bf16[2,64,2048]{2,1,0:T(8,128)(2,1)S(1)} %fusion.33), channel_id=1, source_target_pairs={{24,0},{0,8},{8,16},{16,24},{25,1},{1,9},{9,17},{17,25},{26,2},{2,... | collective-permute-start | bytes 1572872 | tf_op jit(solution)/shard_map/ppermute | solution.py:10
  348.2 52.6 %all-to-all-start.5 = ((bf16[2,8,32,2048]{3,2,0,1:T(8,128)(2,1)}), bf16[2,8,32,2048]{3,2,0,1:T(8,128)(2,1)S(1)}, u32[]{:S(2)}, u32[]{:S(2)}) async-start(bf16[2,8,32,2048]{3,2,0,1:T(8,128)(2,1)} %copy.75), calls=%async_computation.5 | async-start | bytes 4194304 | tf_op jit(solution)/shard_map/all_to_all | solution.py:58
  402.1 14.4 %collective-permute-start.2 = (bf16[2,64,2048]{2,1,0:T(8,128)(2,1)S(1)}, bf16[2,64,2048]{2,1,0:T(8,128)(2,1)S(1)}, u32[]{:S(2)}, u32[]{:S(2)}) collective-permute-start(bf16[2,64,2048]{2,1,0:T(8,128)(2,1)S(1)} %fusion.34), channel_id=1, source_target_pairs={{24,0},{0,8},{8,16},{16,24},{25,1},{1,9},{9,17},{17,25},{26,2},{2,... | collective-permute-start | bytes 1572872 | tf_op jit(solution)/shard_map/ppermute | solution.py:10
  482.2 52.6 %all-to-all-start.7 = ((bf16[2,8,32,2048]{3,2,0,1:T(8,128)(2,1)}), bf16[2,8,32,2048]{3,2,0,1:T(8,128)(2,1)S(1)}, u32[]{:S(2)}, u32[]{:S(2)}) async-start(bf16[2,8,32,2048]{3,2,0,1:T(8,128)(2,1)} %copy.81), calls=%async_computation.7 | async-start | bytes 4194304 | tf_op jit(solution)/shard_map/all_to_all | solution.py:58
  485.9 118.0 %all-reduce.2.cloned.1.call-start = ((), (), s32[]{:S(2)}) async-start(), calls=%async_computation.8 | async-start | bytes 2097152 | tf_op jit(solution)/shard_map/psum | solution.py:15
  537.1 14.4 %collective-permute-start.3 = (bf16[2,64,2048]{2,1,0:T(8,128)(2,1)S(1)}, bf16[2,64,2048]{2,1,0:T(8,128)(2,1)S(1)}, u32[]{:S(2)}, u32[]{:S(2)}) collective-permute-start(bf16[2,64,2048]{2,1,0:T(8,128)(2,1)S(1)} %fusion.35), channel_id=1, source_target_pairs={{24,0},{0,8},{8,16},{16,24},{25,1},{1,9},{9,17},{17,25},{26,2},{2,... | collective-permute-start | bytes 1572872 | tf_op jit(solution)/shard_map/ppermute | solution.py:10
Sparse Core Ops, SparseCore 0:
  552.9 50.9 all-reduce.1
where the time goes:
time: 613 us; the launch traced here: 612 us
  waiting for transfers between devices  297 us (48%)
  blocking collectives  211 us (34%)
  matrix products  46.6 us (8%)
  local copies, waits for them, and re-layouts  19.3 us (3%)
  starting transfers between devices  17.1 us (3%)
  between operations  14.4 us (2%)
  other arithmetic  7.36 us (1%)
    all_to_all x4, blocking collectives, through_exchange(): lax.all_to_all(outgoing, 'expert', split_axis=1, concat_axis=1, tiled=True)  211 us
    all_to_all x4, waiting for transfers between devices, through_exchange(): lax.all_to_all(outputs, 'expert', split_axis=1, concat_axis=1, tiled=True)  192 us
    ppermute x4, waiting for transfers between devices, from_behind(): return lax.ppermute(block, axis, route)  55.1 us
    psum x1, waiting for transfers between devices, spread(): return lax.psum(jnp.where(mine, value, jnp.zeros_like(value)), axis)  50.3 us
    dot_general x4, matrix products, expert_mlp(): jnp.einsum('srf,sfd->srd', activated, down_weight, preferred_element_type...  37.6 us
    all_to_all x4, starting transfers between devices, through_exchange(): lax.all_to_all(outputs, 'expert', split_axis=1, concat_axis=1, tiled=True)  14.7 us
    reshape x4, local copies, waits for them, and re-layouts, through_exchange(): outputs = expert_mlp(shaped, up_weight, down_weight).reshape(in_rows.shape)  12.5 us
  transfers between devices with their start and end apart: 9, of which 9 were waited for; matrix products, arithmetic and copies ran while one was open for 1% of the time, Pallas kernels for 0%

commit v1 on v0

--- a/solution.py
+++ b/solution.py
@@ -1,7 +1,417 @@
+import functools
+
 import jax
 import jax.numpy as jnp
 from jax import lax
+from jax.experimental import pallas as pl
+from jax.experimental.pallas import tpu as pltpu
 from jax.sharding import PartitionSpec as P
+
+EPS = 1e-06
+LANES = 128
+VMEM_LIMIT = 60 * 1024 * 1024
+VMEM_BUDGET = 44 * 1024 * 1024
+MESH = pl.DeviceIdType.MESH
+
+
+def relay_kernel(
+    tick_count, chips, sections, rows, tile,
+    state_ref, gain_ref, up_hbm, down_hbm, ids_ref, gates_ref,
+    final_ref, finished_ref,
+    up, down, layer_in, gathered, partial, from_pair, chain, result, act, row_gate, all_gates,
+    load_sem, gate_send, gate_recv,
+    line_send, line_recv, share_send, share_recv,
+    pair_send, pair_recv, chain_send, chain_recv,
+    hop_send, hop_recv, done_send, done_recv, done_local,
+):
+    width = layer_in.shape[3]
+    hidden = up.shape[2]
+    experts = 2 * chips
+    me = lax.axis_index("expert")
+    place = lax.axis_index("section")
+    chip, core = me // 2, me % 2
+    pair = chip * 2 + 1 - core
+    last = sections - 1
+    columns = width // sections
+
+    loads = [pltpu.make_async_copy(up_hbm.at[c], up.at[c], load_sem.at[c]) for c in range(2)]
+    loads += [pltpu.make_async_copy(down_hbm.at[c], down.at[c], load_sem.at[2 + c]) for c in range(2)]
+    for load in loads:
+        load.start()
+
+    barrier = pltpu.get_barrier_semaphore()
+    for other in range(1, experts):
+        pl.semaphore_signal(
+            barrier, inc=1, device_id={"expert": (me + other) % experts}, device_id_type=MESH)
+    for other in range(1, sections):
+        pl.semaphore_signal(
+            barrier, inc=1, device_id={"section": (place + other) % sections}, device_id_type=MESH)
+
+    def block(index):
+        return pl.ds(pl.multiple_of(index * rows, rows), rows)
+
+    def remote(src, dst, send, recv, to):
+        return pltpu.make_async_remote_copy(
+            src_ref=src, dst_ref=dst, send_sem=send, recv_sem=recv, device_id=to, device_id_type=MESH)
+
+    def gate_copy(other):
+        return remote(all_gates.at[block(me), :], all_gates.at[block(me), :],
+                      gate_send.at[other], gate_recv.at[other], {"expert": (me + other) % experts})
+
+    def line_copy(slot, origin, step):
+        view = gathered.at[slot, block(origin * 2 + core), :]
+        way = 0 if step > 0 else 1
+        return remote(view, view, line_send.at[slot, way, origin], line_recv.at[slot, origin],
+                      {"expert": (chip + step) * 2 + core})
+
+    def share_copy(slot, origin, whose):
+        view = gathered.at[slot, block(origin * 2 + whose), :]
+        return remote(view, view, share_send.at[slot, origin], share_recv.at[slot, origin],
+                      {"expert": pair})
+
+    def pair_copy(slot, target):
+        return remote(partial.at[slot, block(target * 2 + 1 - core), :], from_pair.at[slot, block(target), :],
+                      pair_send.at[slot, target], pair_recv.at[slot, target], {"expert": pair})
+
+    def chain_copy(slot, target, step):
+        way = 0 if step > 0 else 1
+        return remote(partial.at[slot, block(target * 2 + core), :], chain.at[slot, way, block(target), :],
+                      chain_send.at[slot, target], chain_recv.at[slot, way, target],
+                      {"expert": (chip + step) * 2 + core})
+
+    def hop_copy(tick, slot, landing):
+        return remote(result.at[slot], layer_in.at[tick + 1, landing],
+                      hop_send.at[slot], hop_recv.at[tick, landing],
+                      {"section": (place + 1) % sections})
+
+    def done_copy(tick, target):
+        return remote(result.at[1, :, target * columns:(target + 1) * columns], finished_ref.at[tick],
+                      done_send.at[target], done_recv.at[tick], {"section": target})
+
+    def done_keep(tick):
+        return pltpu.make_async_copy(
+            result.at[1, :, last * columns:width], finished_ref.at[tick], done_local)
+
+    chunk = 16
+
+    def norm(tick, slot):
+        @pl.loop(0, rows // chunk)
+        def _(i):
+            at = pl.ds(pl.multiple_of(i * chunk, chunk), chunk)
+            wide = layer_in[tick, slot, at, :].astype(jnp.float32)
+            scale = lax.rsqrt(jnp.mean(wide * wide, axis=-1, keepdims=True) + EPS)
+            into = pl.ds(pl.multiple_of(me * rows + i * chunk, chunk), chunk)
+            gathered[slot, into, :] = (wide * scale * gain_ref[slot][None, :]).astype(jnp.bfloat16)
+
+    def gather_begin(tick, slot):
+        @pl.when(tick > 0)
+        def _():
+            if slot == 0:
+                @pl.when(place == 0)
+                def _():
+                    layer_in[tick, 0] = jnp.zeros((rows, width), jnp.bfloat16)
+
+                @pl.when(place != 0)
+                def _():
+                    hop_copy(tick - 1, slot, slot).wait_recv()
+            else:
+                hop_copy(tick - 1, slot, slot).wait_recv()
+        norm(tick, slot)
+
+        @pl.when(chip < chips - 1)
+        def _():
+            line_copy(slot, chip, 1).start()
+
+        @pl.when(chip > 0)
+        def _():
+            line_copy(slot, chip, -1).start()
+        share_copy(slot, chip, core).start()
+
+    def gather_step(slot, k):
+        for step in (1, -1):
+            origin = chip - step * k
+            inside = origin >= 0 if step > 0 else origin <= chips - 1
+            more = chip < chips - 1 if step > 0 else chip > 0
+
+            @pl.when(inside)
+            def _():
+                line_copy(slot, origin, step).wait_recv()
+
+                @pl.when(more)
+                def _():
+                    line_copy(slot, origin, step).start()
+                share_copy(slot, origin, core).start()
+
+    def gather_end(slot):
+        for origin in range(chips):
+            share_copy(slot, origin, 1 - core).wait_recv()
+
+    def gather_drain(slot):
+        for origin in range(chips):
+            share_copy(slot, origin, core).wait_send()
+
+            @pl.when((origin <= chip) & (chip < chips - 1))
+            def _():
+                line_copy(slot, origin, 1).wait_send()
+
+            @pl.when((origin >= chip) & (chip > 0))
+            def _():
+                line_copy(slot, origin, -1).wait_send()
+
+    def scatter_drain(slot):
+        for target in range(chips):
+            pair_copy(slot, target).wait_send()
+
+            @pl.when(target != chip)
+            def _():
+                chain_copy(slot, target, 1).wait_send()
+
+    def compute(tick, slot):
+        @pl.when(tick > 0)
+        def _():
+            scatter_drain(slot)
+        total = experts * rows
+        lane = lax.broadcasted_iota(jnp.int32, (rows, LANES), 1)
+        here = (lane // 2) == (tick * 2 + slot)
+
+        @pl.loop(0, experts)
+        def _(j):
+            chosen = jnp.where(here & (ids_ref[block(j), :] == me), all_gates[block(j), :], 0.0)
+            row_gate[block(j), :] = jnp.broadcast_to(
+                jnp.sum(chosen, axis=1, keepdims=True), (rows, tile))
+
+        @pl.loop(0, hidden // tile)
+        def _(n):
+            at = pl.ds(pl.multiple_of(n * tile, tile), tile)
+            lifted = jnp.dot(gathered[slot], up[slot, :, at], preferred_element_type=jnp.float32)
+            act[:, at] = (lifted / (1.0 + jnp.exp(-lifted))).astype(jnp.bfloat16)
+
+        @pl.loop(0, width // tile)
+        def _(n):
+            at = pl.ds(pl.multiple_of(n * tile, tile), tile)
+            lowered = jnp.dot(act[...], down[slot, :, at], preferred_element_type=jnp.float32)
+            partial[slot, :, at] = (lowered * row_gate[...]).astype(jnp.bfloat16)
+        gather_drain(slot)
+        for target in range(chips):
+            pair_copy(slot, target).start()
+
+    def add_to(slot, target, ways):
+        mine = target * 2 + core
+
+        @pl.loop(0, rows // chunk)
+        def _(i):
+            own = pl.ds(pl.multiple_of(mine * rows + i * chunk, chunk), chunk)
+            there = pl.ds(pl.multiple_of(target * rows + i * chunk, chunk), chunk)
+            total = partial[slot, own, :].astype(jnp.float32) + from_pair[slot, there, :].astype(jnp.float32)
+            for way in ways:
+                total += chain[slot, way, there, :].astype(jnp.float32)
+            partial[slot, own, :] = total.astype(jnp.bfloat16)
+
+    def scatter_send(slot, target, step, first):
+        pair_copy(slot, target).wait_recv()
+        if not first:
+            chain_copy(slot, target, step).wait_recv()
+        add_to(slot, target, () if first else ((0,) if step > 0 else (1,)))
+        chain_copy(slot, target, step).start()
+
+    def scatter_begin(slot):
+        @pl.when(chip == 0)
+        def _():
+            for target in range(chips - 1, 0, -1):
+                scatter_send(slot, target, 1, True)
+
+        @pl.when(chip == chips - 1)
+        def _():
+            for target in range(chips - 1):
+                scatter_send(slot, target, -1, True)
+
+    def scatter_step(slot, k):
+        @pl.when((chips - k > chip) & (chip > 0))
+        def _():
+            scatter_send(slot, chips - k, 1, False)
+
+        @pl.when((k - 1 < chip) & (chip < chips - 1))
+        def _():
+            scatter_send(slot, k - 1, -1, False)
+
+    def scatter_end(tick, slot):
+        pair_copy(slot, chip).wait_recv()
+
+        @pl.when(chip > 0)
+        def _():
+            chain_copy(slot, chip, 1).wait_recv()
+
+        @pl.when(chip < chips - 1)
+        def _():
+            chain_copy(slot, chip, -1).wait_recv()
+
+        @pl.when(chip == 0)
+        def _():
+            add_to(slot, chip, (1,))
+
+        @pl.when(chip == chips - 1)
+        def _():
+            add_to(slot, chip, (0,))
+
+        @pl.when((chip > 0) & (chip < chips - 1))
+        def _():
+            add_to(slot, chip, (0, 1))
+
+        @pl.when(tick > 0)
+        def _():
+            hop_drain(slot)
+
+        @pl.loop(0, rows // chunk)
+        def _(i):
+            own = pl.ds(pl.multiple_of(me * rows + i * chunk, chunk), chunk)
+            at = pl.ds(pl.multiple_of(i * chunk, chunk), chunk)
+            total = partial[slot, own, :].astype(jnp.float32) + layer_in[tick, slot, at, :].astype(jnp.float32)
+            result[slot, at, :] = total.astype(jnp.bfloat16)
+
+        @pl.when(place < last)
+        def _():
+            hop_copy(tick, slot, slot).start()
+
+        @pl.when(place == last)
+        def _():
+            if slot == 0:
+                hop_copy(tick, 0, 1).start()
+            else:
+                for target in range(last):
+                    done_copy(tick, target).start()
+                done_keep(tick).start()
+
+    def hop_drain(slot):
+        if slot == 0:
+            hop_copy(0, 0, 0).wait_send()
+        else:
+            @pl.when(place < last)
+            def _():
+                hop_copy(0, 1, 1).wait_send()
+
+            @pl.when(place == last)
+            def _():
+                for target in range(last):
+                    done_copy(0, target).wait_send()
+                done_keep(0).wait()
+
+    layer_in[0] = state_ref[...]
+    all_gates[block(me), :] = gates_ref[...]
+    pl.semaphore_wait(barrier, experts - 1 + sections - 1)
+    def half(tick, slot, other_tick, other):
+        gather_begin(tick, slot)
+        scatter_begin(other)
+        for k in range(1, chips):
+            gather_step(slot, k)
+            scatter_step(other, k)
+        scatter_end(other_tick, other)
+        gather_end(slot)
+        compute(tick, slot)
+
+    gather_begin(0, 0)
+    for other in range(1, experts):
+        gate_copy(other).start()
+    for k in range(1, chips):
+        gather_step(0, k)
+    gather_end(0)
+    for load in loads:
+        load.wait()
+    for other in range(1, experts):
+        gate_copy(other).wait_recv()
+    compute(0, 0)
+
+    half(0, 1, 0, 0)
+
+    @pl.loop(1, tick_count)
+    def _(tick):
+        half(tick, 0, tick - 1, 1)
+        half(tick, 1, tick, 0)
+
+    scatter_begin(1)
+    for k in range(1, chips):
+        scatter_step(1, k)
+    scatter_end(tick_count - 1, 1)
+
+    for slot in range(2):
+        scatter_drain(slot)
+        hop_drain(slot)
+    for other in range(1, experts):
+        gate_copy(other).wait_send()
+
+    @pl.when(place == 0)
+    def _():
+        layer_in[tick_count, 0] = jnp.zeros((rows, width), jnp.bfloat16)
+
+    @pl.when(place != 0)
+    def _():
+        hop_copy(tick_count - 1, 0, 0).wait_recv()
+    hop_copy(tick_count - 1, 1, 1).wait_recv()
+
+    @pl.when(place != last)
+    def _():
+        for tick in range(tick_count):
+            done_copy(tick, 0).wait_recv()
+    final_ref[...] = layer_in[tick_count]
+
+
+def tile_of(width, hidden):
+    for tile in (256, 128):
+        if width % tile == 0 and hidden % tile == 0:
+            return tile
+    return 0
+
+
+def relay_bytes(ticks, experts, rows, width, hidden):
+    weights = 2 * 2 * width * hidden * 2
+    per_block = rows * width * 2
+    blocks = 2 * (ticks + 1) + 2 * experts * 2 + experts + 2 * experts + 2 + 4
+    return weights + blocks * per_block + experts * rows * (hidden * 2 + 2 * LANES * 4 + 2 * LANES * 4)
+
+
+def on_device_relay(tick_count, experts, sections, tile, state, norm_gain, up_weight, down_weight, expert_ids, gate_values):
+    rows, width = state.shape[2], state.shape[3]
+    hidden = up_weight.shape[4]
+    chips = experts // 2
+    routes = jnp.transpose(expert_ids[:, :, 0], (2, 0, 1, 3)).reshape(experts * rows, tick_count * 4)
+    gates = jnp.transpose(gate_values[:, :, 0], (1 + 1, 0, 1, 3)).reshape(rows, tick_count * 4)
+    routes = jnp.pad(routes, ((0, 0), (0, LANES - tick_count * 4)))
+    gates = jnp.pad(gates, ((0, 0), (0, LANES - tick_count * 4)))
+    vmem = pl.BlockSpec(memory_space=pltpu.VMEM)
+    hbm = pl.BlockSpec(memory_space=pl.ANY)
+    bf16 = jnp.bfloat16
+    dma = pltpu.SemaphoreType.DMA
+    final, finished = pl.pallas_call(
+        functools.partial(relay_kernel, tick_count, chips, sections, rows, tile),
+        out_shape=(
+            jax.ShapeDtypeStruct((2, rows, width), bf16),
+            jax.ShapeDtypeStruct((tick_count, rows, width // sections), bf16),
+        ),
+        in_specs=[vmem, vmem, hbm, hbm, vmem, vmem],
+        out_specs=(vmem, vmem),
+        scratch_shapes=[
+            pltpu.VMEM((2, width, hidden), bf16),
+            pltpu.VMEM((2, hidden, width), bf16),
+            pltpu.VMEM((tick_count + 1, 2, rows, width), bf16),
+            pltpu.VMEM((2, experts * rows, width), bf16),
+            pltpu.VMEM((2, experts * rows, width), bf16),
+            pltpu.VMEM((2, chips * rows, width), bf16),
+            pltpu.VMEM((2, 2, chips * rows, width), bf16),
+            pltpu.VMEM((2, rows, width), bf16),
+            pltpu.VMEM((experts * rows, hidden), bf16),
+            pltpu.VMEM((experts * rows, tile), jnp.float32),
+            pltpu.VMEM((experts * rows, LANES), jnp.float32),
+            dma((4,)), dma((experts,)), dma((experts,)),
+            dma((2, 2, chips)), dma((2, chips)), dma((2, chips)), dma((2, chips)),
+            dma((2, chips)), dma((2, chips)), dma((2, chips)), dma((2, 2, chips)),
+            dma((2,)), dma((tick_count, 2)), dma((sections,)), dma((tick_count,)), dma(()),
+        ],
+        compiler_params=pltpu.CompilerParams(
+            collective_id=0, has_side_effects=True, vmem_limit_bytes=VMEM_LIMIT),
+        cost_estimate=pl.CostEstimate(
+            flops=tick_count * 2 * experts * rows * width * hidden * 4,
+            bytes_accessed=8 * width * hidden, transcendentals=0),
+    )(state[:, 0], norm_gain[:, 0], up_weight[:, 0, 0], down_weight[:, 0, 0], routes, gates)
+    return final[:, None], finished
 
 
 def from_behind(block, axis, distance):
@@ -39,9 +449,12 @@
     own_routes = lax.dynamic_slice_in_dim(routes, owner * tok_rows, tok_rows, 1)
     matches = (own_routes[..., None] == jnp.arange(expert_count, dtype=jnp.int32)).astype(jnp.int32)
     flattened = matches.reshape(slot_count, tok_rows * 2, expert_count)
-    earlier = (jnp.cumsum(flattened, axis=1) - flattened).reshape(
-        slot_count, tok_rows, 2, expert_count
+    picks = jnp.arange(tok_rows * 2)
+    before = (picks[:, None] > picks[None, :]).astype(jnp.bfloat16)
+    earlier = jnp.einsum(
+        "ab,sbe->sae", before, flattened.astype(jnp.bfloat16), preferred_element_type=jnp.float32
     )
+    earlier = earlier.astype(jnp.int32).reshape(slot_count, tok_rows, 2, expert_count)
     position = jnp.sum(earlier * matches, axis=3)
     slot_match = (position[..., None, None] == jnp.arange(per_source, dtype=jnp.int32)).astype(
         jnp.int32
@@ -97,17 +510,33 @@
 
 
 def solution(mesh):
-    return jax.shard_map(
-        on_device,
-        mesh=mesh,
-        in_specs=(
-            P(None, "section", "expert", None),
-            P(None, "section", None),
-            P(None, "section", "expert", None, None),
-            P(None, "section", "expert", None, None),
-            P(None, None, "section", None, None),
-            P(None, None, "section", "expert", None),
-        ),
-        out_specs=(P(None, "section", "expert", None), P(None, "expert", "section")),
-        check_vma=False,
-    )
+    experts, sections = mesh.shape["expert"], mesh.shape["section"]
+
+    def whole(state, norm_gain, up_weight, down_weight, expert_ids, gate_values):
+        ticks = expert_ids.shape[0]
+        rows, width, hidden = state.shape[2] // experts, state.shape[3], up_weight.shape[4]
+        tile = tile_of(width, hidden)
+        fits = (
+            experts % 2 == 0 and experts >= 4 and sections >= 2 and rows % 16 == 0 and tile
+            and width % (sections * LANES) == 0 and ticks * 4 <= LANES
+            and relay_bytes(ticks, experts, rows, width, hidden) <= VMEM_BUDGET
+        )
+        body = on_device
+        if fits:
+            body = functools.partial(on_device_relay, ticks, experts, sections, tile)
+        return jax.shard_map(
+            body,
+            mesh=mesh,
+            in_specs=(
+                P(None, "section", "expert", None),
+                P(None, "section", None),
+                P(None, "section", "expert", None, None),
+                P(None, "section", "expert", None, None),
+                P(None, None, "section", None, None),
+                P(None, None, "section", "expert", None),
+            ),
+            out_specs=(P(None, "section", "expert", None), P(None, "expert", "section")),
+            check_vma=False,
+        )(state, norm_gain, up_weight, down_weight, expert_ids, gate_values)
+
+    return whole

time: 613 us -> 423 us (0.69)
  Pallas kernels: 0 us -> 414 us
  waiting for transfers between devices: 297 us -> 0 us
  blocking collectives: 211 us -> 0 us
  matrix products: 46.6 us -> 0 us
  starting transfers between devices: 17.1 us -> 0 us
  between operations: 14.4 us -> 0.65 us
  local copies, waits for them, and re-layouts: 19.3 us -> 7.91 us
  other arithmetic: 7.36 us -> 0 us
    pallas_call x0 -> x1, Pallas kernels: none -> 414 us  [on_device_relay(): pl.pallas_call(functools.partial(relay_kernel, tick_count, chips, section...]
    all_to_all x4 -> x0, blocking collectives: 211 us -> none  [through_exchange(): lax.all_to_all(outgoing, 'expert', split_axis=1, concat_axis=1, tiled=True)]
    all_to_all x4 -> x0, waiting for transfers between devices: 192 us -> none  [through_exchange(): lax.all_to_all(outputs, 'expert', split_axis=1, concat_axis=1, tiled=True)]
    ppermute x4 -> x0, waiting for transfers between devices: 55.1 us -> none  [from_behind(): return lax.ppermute(block, axis, route)]
    psum x1 -> x0, waiting for transfers between devices: 50.3 us -> none  [spread(): return lax.psum(jnp.where(mine, value, jnp.zeros_like(value)), axis)]
    dot_general x12 -> x0, matrix products: 46.6 us -> none  [the longest x4 37.6 us: expert_mlp(): jnp.einsum('srf,sfd->srd', activated, down_weight, preferred_element_type...]
    all_to_all x4 -> x0, starting transfers between devices: 14.7 us -> none  [through_exchange(): lax.all_to_all(outputs, 'expert', split_axis=1, concat_axis=1, tiled=True)]
    reshape x4 -> x3, local copies, waits for them, and re-layouts: 12.5 us -> 1.68 us  [the longest x2 0.9 us: on_device_relay(): jnp.transpose(expert_ids[:, :, 0], (2, 0, 1, 3))]
  transfers between devices with their start and end apart: 9 -> 0, of which waited for: 9 -> 0; matrix products, arithmetic and copies ran while one was open for 1% -> 0% of each run, Pallas kernels for 0% -> 0%
where the time goes in v1:
time: 423 us
  Pallas kernels  414 us (98%)
  local copies, waits for them, and re-layouts  7.91 us (2%)
    pallas_call x1, Pallas kernels, on_device_relay(): pl.pallas_call(functools.partial(relay_kernel, tick_count, chips, section...  414 us

profile of v1, /device:TPU:0, one launch (start us, length us, event | category | flops | bytes accessed | tf_op | source)
XLA Modules:
  0.0 422.9 jit_solution(15932103731314490087)
XLA Ops:
  0.6 1.3 copy.16
  2.0 0.8 reshape.10
  2.7 0.8 copy.12
  3.5 0.6 pad.9.gates_ref
  4.1 0.1 copy.11
  4.3 0.7 pad.8.ids_ref
  5.0 414.3 %shard_map.77 = (bf16[2,64,2048]{2,1,0:T(8,128)(2,1)}, bf16[4,64,512]{2,1,0:T(8,128)(2,1)}) custom-call(bf16[2,64,2048]{2,1,0:T(8,128)(2,1)} %bitcast.25, f32[2,2048]{1,0:T(2,128)} %bitcast.21, bf16[2,2048,768]{2,1,0:T(8,128)(2,1)} %bitcast.23, bf16[2,768,2048]{2,1,0:T(8,128)(2,1)} %bitcast.24, s32[512,128]{1,0:T(8,128)} %pad.8.ids_ref, f32[64,128]{1,0:T(8,128)} %pad.9.gates_ref), custom_call_target="tpu_custom_call" | custom-call | flops 25769803776 | bytes 12582912 | tf_op jit(solution)/shard_map/pallas_call | solution.py:383
  419.3 1.9 copy.19
  421.2 1.7 copy.20

commit v2 on v1

--- a/solution.py
+++ b/solution.py
@@ -47,6 +47,13 @@
         pl.semaphore_signal(
             barrier, inc=1, device_id={"section": (place + other) % sections}, device_id_type=MESH)
 
+    chunk = 16
+    halves = 2 if rows % (2 * chunk) == 0 else 1
+    sub = rows // halves
+
+    def part(index, h):
+        return pl.ds(pl.multiple_of(index * rows + h * sub, sub), sub)
+
     def block(index):
         return pl.ds(pl.multiple_of(index * rows, rows), rows)
 
@@ -58,10 +65,10 @@
         return remote(all_gates.at[block(me), :], all_gates.at[block(me), :],
                       gate_send.at[other], gate_recv.at[other], {"expert": (me + other) % experts})
 
-    def line_copy(slot, origin, step):
-        view = gathered.at[slot, block(origin * 2 + core), :]
+    def line_copy(slot, origin, step, h):
+        view = gathered.at[slot, part(origin * 2 + core, h), :]
         way = 0 if step > 0 else 1
-        return remote(view, view, line_send.at[slot, way, origin], line_recv.at[slot, origin],
+        return remote(view, view, line_send.at[slot, way, origin, h], line_recv.at[slot, origin, h],
                       {"expert": (chip + step) * 2 + core})
 
     def share_copy(slot, origin, whose):
@@ -73,15 +80,15 @@
         return remote(partial.at[slot, block(target * 2 + 1 - core), :], from_pair.at[slot, block(target), :],
                       pair_send.at[slot, target], pair_recv.at[slot, target], {"expert": pair})
 
-    def chain_copy(slot, target, step):
+    def chain_copy(slot, target, step, h):
         way = 0 if step > 0 else 1
-        return remote(partial.at[slot, block(target * 2 + core), :], chain.at[slot, way, block(target), :],
-                      chain_send.at[slot, target], chain_recv.at[slot, way, target],
+        return remote(partial.at[slot, part(target * 2 + core, h), :], chain.at[slot, way, part(target, h), :],
+                      chain_send.at[slot, target, h], chain_recv.at[slot, way, target, h],
                       {"expert": (chip + step) * 2 + core})
 
-    def hop_copy(tick, slot, landing):
-        return remote(result.at[slot], layer_in.at[tick + 1, landing],
-                      hop_send.at[slot], hop_recv.at[tick, landing],
+    def hop_copy(tick, slot, landing, h):
+        return remote(result.at[slot, part(0, h), :], layer_in.at[tick + 1, landing, part(0, h), :],
+                      hop_send.at[slot, h], hop_recv.at[tick, landing, h],
                       {"section": (place + 1) % sections})
 
     def done_copy(tick, target):
@@ -92,42 +99,44 @@
         return pltpu.make_async_copy(
             result.at[1, :, last * columns:width], finished_ref.at[tick], done_local)
 
-    chunk = 16
-
-    def norm(tick, slot):
-        @pl.loop(0, rows // chunk)
+    def norm(tick, slot, h):
+        @pl.loop(0, sub // chunk)
         def _(i):
-            at = pl.ds(pl.multiple_of(i * chunk, chunk), chunk)
+            at = pl.ds(pl.multiple_of(h * sub + i * chunk, chunk), chunk)
             wide = layer_in[tick, slot, at, :].astype(jnp.float32)
             scale = lax.rsqrt(jnp.mean(wide * wide, axis=-1, keepdims=True) + EPS)
-            into = pl.ds(pl.multiple_of(me * rows + i * chunk, chunk), chunk)
+            into = pl.ds(pl.multiple_of(me * rows + h * sub + i * chunk, chunk), chunk)
             gathered[slot, into, :] = (wide * scale * gain_ref[slot][None, :]).astype(jnp.bfloat16)
 
+    def hop_arrive(tick, slot, h):
+        if slot == 0:
+            @pl.when(place == 0)
+            def _():
+                layer_in[tick, 0, h * sub:(h + 1) * sub, :] = jnp.zeros((sub, width), jnp.bfloat16)
+
+            @pl.when(place != 0)
+            def _():
+                hop_copy(tick - 1, slot, slot, h).wait_recv()
+        else:
+            hop_copy(tick - 1, slot, slot, h).wait_recv()
+
     def gather_begin(tick, slot):
-        @pl.when(tick > 0)
-        def _():
-            if slot == 0:
-                @pl.when(place == 0)
-                def _():
-                    layer_in[tick, 0] = jnp.zeros((rows, width), jnp.bfloat16)
-
-                @pl.when(place != 0)
-                def _():
-                    hop_copy(tick - 1, slot, slot).wait_recv()
-            else:
-                hop_copy(tick - 1, slot, slot).wait_recv()
-        norm(tick, slot)
-
-        @pl.when(chip < chips - 1)
-        def _():
-            line_copy(slot, chip, 1).start()
-
-        @pl.when(chip > 0)
-        def _():
-            line_copy(slot, chip, -1).start()
+        for h in range(halves):
+            @pl.when(tick > 0)
+            def _():
+                hop_arrive(tick, slot, h)
+            norm(tick, slot, h)
+
+            @pl.when(chip < chips - 1)
+            def _():
+                line_copy(slot, chip, 1, h).start()
+
+            @pl.when(chip > 0)
+            def _():
+                line_copy(slot, chip, -1, h).start()
         share_copy(slot, chip, core).start()
 
-    def gather_step(slot, k):
+    def gather_step(slot, k, h):
         for step in (1, -1):
             origin = chip - step * k
             inside = origin >= 0 if step > 0 else origin <= chips - 1
@@ -135,12 +144,13 @@
 
             @pl.when(inside)
             def _():
-                line_copy(slot, origin, step).wait_recv()
+                line_copy(slot, origin, step, h).wait_recv()
 
                 @pl.when(more)
                 def _():
-                    line_copy(slot, origin, step).start()
-                share_copy(slot, origin, core).start()
+                    line_copy(slot, origin, step, h).start()
+                if h == halves - 1:
+                    share_copy(slot, origin, core).start()
 
     def gather_end(slot):
         for origin in range(chips):
@@ -149,14 +159,14 @@
     def gather_drain(slot):
         for origin in range(chips):
             share_copy(slot, origin, core).wait_send()
-
-            @pl.when((origin <= chip) & (chip < chips - 1))
-            def _():
-                line_copy(slot, origin, 1).wait_send()
-
-            @pl.when((origin >= chip) & (chip > 0))
-            def _():
-                line_copy(slot, origin, -1).wait_send()
+            for h in range(halves):
+                @pl.when((origin <= chip) & (chip < chips - 1))
+                def _():
+                    line_copy(slot, origin, 1, h).wait_send()
+
+                @pl.when((origin >= chip) & (chip > 0))
+                def _():
+                    line_copy(slot, origin, -1, h).wait_send()
 
     def scatter_drain(slot):
         for target in range(chips):
@@ -164,13 +174,10 @@
 
             @pl.when(target != chip)
             def _():
-                chain_copy(slot, target, 1).wait_send()
-
-    def compute(tick, slot):
-        @pl.when(tick > 0)
-        def _():
-            scatter_drain(slot)
-        total = experts * rows
+                for h in range(halves):
+                    chain_copy(slot, target, 1, h).wait_send()
+
+    def compute_up(tick, slot):
         lane = lax.broadcasted_iota(jnp.int32, (rows, LANES), 1)
         here = (lane // 2) == (tick * 2 + slot)
 
@@ -185,109 +192,113 @@
             at = pl.ds(pl.multiple_of(n * tile, tile), tile)
             lifted = jnp.dot(gathered[slot], up[slot, :, at], preferred_element_type=jnp.float32)
             act[:, at] = (lifted / (1.0 + jnp.exp(-lifted))).astype(jnp.bfloat16)
+        gather_drain(slot)
+
+    def compute_down(tick, slot):
+        @pl.when(tick > 0)
+        def _():
+            scatter_drain(slot)
 
         @pl.loop(0, width // tile)
         def _(n):
             at = pl.ds(pl.multiple_of(n * tile, tile), tile)
             lowered = jnp.dot(act[...], down[slot, :, at], preferred_element_type=jnp.float32)
             partial[slot, :, at] = (lowered * row_gate[...]).astype(jnp.bfloat16)
-        gather_drain(slot)
         for target in range(chips):
             pair_copy(slot, target).start()
 
-    def add_to(slot, target, ways):
-        mine = target * 2 + core
-
-        @pl.loop(0, rows // chunk)
+    def summed(slot, target, ways, start):
+        own = pl.ds(pl.multiple_of(target * 2 * rows + core * rows + start, chunk), chunk)
+        there = pl.ds(pl.multiple_of(target * rows + start, chunk), chunk)
+        total = partial[slot, own, :].astype(jnp.float32) + from_pair[slot, there, :].astype(jnp.float32)
+        for way in ways:
+            total += chain[slot, way, there, :].astype(jnp.float32)
+        return own, total
+
+    def add_to(slot, target, ways, h):
+        @pl.loop(0, sub // chunk)
         def _(i):
-            own = pl.ds(pl.multiple_of(mine * rows + i * chunk, chunk), chunk)
-            there = pl.ds(pl.multiple_of(target * rows + i * chunk, chunk), chunk)
-            total = partial[slot, own, :].astype(jnp.float32) + from_pair[slot, there, :].astype(jnp.float32)
-            for way in ways:
-                total += chain[slot, way, there, :].astype(jnp.float32)
+            own, total = summed(slot, target, ways, h * sub + i * chunk)
             partial[slot, own, :] = total.astype(jnp.bfloat16)
 
-    def scatter_send(slot, target, step, first):
-        pair_copy(slot, target).wait_recv()
-        if not first:
-            chain_copy(slot, target, step).wait_recv()
-        add_to(slot, target, () if first else ((0,) if step > 0 else (1,)))
-        chain_copy(slot, target, step).start()
-
-    def scatter_begin(slot):
-        @pl.when(chip == 0)
-        def _():
-            for target in range(chips - 1, 0, -1):
-                scatter_send(slot, target, 1, True)
-
-        @pl.when(chip == chips - 1)
-        def _():
-            for target in range(chips - 1):
-                scatter_send(slot, target, -1, True)
-
-    def scatter_step(slot, k):
-        @pl.when((chips - k > chip) & (chip > 0))
-        def _():
-            scatter_send(slot, chips - k, 1, False)
-
-        @pl.when((k - 1 < chip) & (chip < chips - 1))
-        def _():
-            scatter_send(slot, k - 1, -1, False)
+    def finish(tick, slot, ways, h):
+        @pl.loop(0, sub // chunk)
+        def _(i):
+            _, total = summed(slot, chip, ways, h * sub + i * chunk)
+            at = pl.ds(pl.multiple_of(h * sub + i * chunk, chunk), chunk)
+            result[slot, at, :] = (total + layer_in[tick, slot, at, :].astype(jnp.float32)).astype(jnp.bfloat16)
+
+    def scatter_step(slot, turn, h):
+        for step in (1, -1):
+            target = chip + step * (chips - turn + 1)
+            inside = (target <= chips - 1) if step > 0 else (target >= 0)
+            first = chip == 0 if step > 0 else chip == chips - 1
+
+            @pl.when(inside)
+            def _():
+                if h == 0:
+                    pair_copy(slot, target).wait_recv()
+
+                @pl.when(first)
+                def _():
+                    add_to(slot, target, (), h)
+
+                @pl.when(jnp.logical_not(first))
+                def _():
+                    chain_copy(slot, target, step, h).wait_recv()
+                    add_to(slot, target, (0,) if step > 0 else (1,), h)
+                chain_copy(slot, target, step, h).start()
 
     def scatter_end(tick, slot):
         pair_copy(slot, chip).wait_recv()
-
-        @pl.when(chip > 0)
-        def _():
-            chain_copy(slot, chip, 1).wait_recv()
-
-        @pl.when(chip < chips - 1)
-        def _():
-            chain_copy(slot, chip, -1).wait_recv()
-
-        @pl.when(chip == 0)
-        def _():
-            add_to(slot, chip, (1,))
-
-        @pl.when(chip == chips - 1)
-        def _():
-            add_to(slot, chip, (0,))
-
-        @pl.when((chip > 0) & (chip < chips - 1))
-        def _():
-            add_to(slot, chip, (0, 1))
 
         @pl.when(tick > 0)
         def _():
             hop_drain(slot)
-
-        @pl.loop(0, rows // chunk)
-        def _(i):
-            own = pl.ds(pl.multiple_of(me * rows + i * chunk, chunk), chunk)
-            at = pl.ds(pl.multiple_of(i * chunk, chunk), chunk)
-            total = partial[slot, own, :].astype(jnp.float32) + layer_in[tick, slot, at, :].astype(jnp.float32)
-            result[slot, at, :] = total.astype(jnp.bfloat16)
-
-        @pl.when(place < last)
-        def _():
-            hop_copy(tick, slot, slot).start()
-
-        @pl.when(place == last)
-        def _():
+        for h in range(halves):
+            @pl.when(chip > 0)
+            def _():
+                chain_copy(slot, chip, 1, h).wait_recv()
+
+            @pl.when(chip < chips - 1)
+            def _():
+                chain_copy(slot, chip, -1, h).wait_recv()
+
+            @pl.when(chip == 0)
+            def _():
+                finish(tick, slot, (1,), h)
+
+            @pl.when(chip == chips - 1)
+            def _():
+                finish(tick, slot, (0,), h)
+
+            @pl.when((chip > 0) & (chip < chips - 1))
+            def _():
+                finish(tick, slot, (0, 1), h)
+
+            @pl.when(place < last)
+            def _():
+                hop_copy(tick, slot, slot, h).start()
             if slot == 0:
-                hop_copy(tick, 0, 1).start()
-            else:
+                @pl.when(place == last)
+                def _():
+                    hop_copy(tick, 0, 1, h).start()
+        if slot == 1:
+            @pl.when(place == last)
+            def _():
                 for target in range(last):
                     done_copy(tick, target).start()
                 done_keep(tick).start()
 
     def hop_drain(slot):
         if slot == 0:
-            hop_copy(0, 0, 0).wait_send()
+            for h in range(halves):
+                hop_copy(0, 0, 0, h).wait_send()
         else:
             @pl.when(place < last)
             def _():
-                hop_copy(0, 1, 1).wait_send()
+                for h in range(halves):
+                    hop_copy(0, 1, 1, h).wait_send()
 
             @pl.when(place == last)
             def _():
@@ -295,30 +306,35 @@
                     done_copy(0, target).wait_send()
                 done_keep(0).wait()
 
+    def half(tick, slot, other_tick, other):
+        gather_begin(tick, slot)
+        for turn in range(1, chips + 1):
+            for h in range(halves):
+                if turn > 1:
+                    gather_step(slot, turn - 1, h)
+                    scatter_step(other, turn, h)
+        gather_end(slot)
+        compute_up(tick, slot)
+        scatter_end(other_tick, other)
+        compute_down(tick, slot)
+
     layer_in[0] = state_ref[...]
     all_gates[block(me), :] = gates_ref[...]
     pl.semaphore_wait(barrier, experts - 1 + sections - 1)
-    def half(tick, slot, other_tick, other):
-        gather_begin(tick, slot)
-        scatter_begin(other)
-        for k in range(1, chips):
-            gather_step(slot, k)
-            scatter_step(other, k)
-        scatter_end(other_tick, other)
-        gather_end(slot)
-        compute(tick, slot)
 
     gather_begin(0, 0)
     for other in range(1, experts):
         gate_copy(other).start()
     for k in range(1, chips):
-        gather_step(0, k)
+        for h in range(halves):
+            gather_step(0, k, h)
     gather_end(0)
     for load in loads:
         load.wait()
     for other in range(1, experts):
         gate_copy(other).wait_recv()
-    compute(0, 0)
+    compute_up(0, 0)
+    compute_down(0, 0)
 
     half(0, 1, 0, 0)
 
@@ -327,9 +343,9 @@
         half(tick, 0, tick - 1, 1)
         half(tick, 1, tick, 0)
 
-    scatter_begin(1)
-    for k in range(1, chips):
-        scatter_step(1, k)
+    for turn in range(2, chips + 1):
+        for h in range(halves):
+            scatter_step(1, turn, h)
     scatter_end(tick_count - 1, 1)
 
     for slot in range(2):
@@ -337,15 +353,9 @@
         hop_drain(slot)
     for other in range(1, experts):
         gate_copy(other).wait_send()
-
-    @pl.when(place == 0)
-    def _():
-        layer_in[tick_count, 0] = jnp.zeros((rows, width), jnp.bfloat16)
-
-    @pl.when(place != 0)
-    def _():
-        hop_copy(tick_count - 1, 0, 0).wait_recv()
-    hop_copy(tick_count - 1, 1, 1).wait_recv()
+    for h in range(halves):
+        hop_arrive(tick_count, 0, h)
+        hop_arrive(tick_count, 1, h)
 
     @pl.when(place != last)
     def _():
@@ -401,9 +411,9 @@
             pltpu.VMEM((experts * rows, tile), jnp.float32),
             pltpu.VMEM((experts * rows, LANES), jnp.float32),
             dma((4,)), dma((experts,)), dma((experts,)),
-            dma((2, 2, chips)), dma((2, chips)), dma((2, chips)), dma((2, chips)),
-            dma((2, chips)), dma((2, chips)), dma((2, chips)), dma((2, 2, chips)),
-            dma((2,)), dma((tick_count, 2)), dma((sections,)), dma((tick_count,)), dma(()),
+            dma((2, 2, chips, 2)), dma((2, chips, 2)), dma((2, chips)), dma((2, chips)),
+            dma((2, chips)), dma((2, chips)), dma((2, chips, 2)), dma((2, 2, chips, 2)),
+            dma((2, 2)), dma((tick_count, 2, 2)), dma((sections,)), dma((tick_count,)), dma(()),
         ],
         compiler_params=pltpu.CompilerParams(
             collective_id=0, has_side_effects=True, vmem_limit_bytes=VMEM_LIMIT),

time: 423 us -> 269 us (0.64)
  Pallas kernels: 414 us -> 260 us
    pallas_call x1, Pallas kernels: 414 us -> 260 us  [on_device_relay(): pl.pallas_call(functools.partial(relay_kernel, tick_count, chips, section...]
where the time goes in v2:
time: 269 us; the launch traced here: 268 us
  Pallas kernels  260 us (97%)
  local copies, waits for them, and re-layouts  7.91 us (3%)
    pallas_call x1, Pallas kernels, on_device_relay(): pl.pallas_call(functools.partial(relay_kernel, tick_count, chips, section...  260 us

profile of v2, /device:TPU:0, one launch (start us, length us, event | category | flops | bytes accessed | tf_op | source)
XLA Modules:
  0.0 268.4 jit_solution(7589833819006912372)
XLA Ops:
  0.6 1.3 copy.16
  2.0 0.8 reshape.10
  2.7 0.8 copy.12
  3.5 0.6 pad.9.gates_ref
  4.1 0.1 copy.11
  4.3 0.7 pad.8.ids_ref
  5.0 259.8 %shard_map.77 = (bf16[2,64,2048]{2,1,0:T(8,128)(2,1)}, bf16[4,64,512]{2,1,0:T(8,128)(2,1)}) custom-call(bf16[2,64,2048]{2,1,0:T(8,128)(2,1)} %bitcast.25, f32[2,2048]{1,0:T(2,128)} %bitcast.21, bf16[2,2048,768]{2,1,0:T(8,128)(2,1)} %bitcast.23, bf16[2,768,2048]{2,1,0:T(8,128)(2,1)} %bitcast.24, s32[512,128]{1,0:T(8,128)} %pad.8.ids_ref, f32[64,128]{1,0:T(8,128)} %pad.9.gates_ref), custom_call_target="tpu_custom_call" | custom-call | flops 25769803776 | bytes 12582912 | tf_op jit(solution)/shard_map/pallas_call | solution.py:393
  264.8 1.9 copy.19
  266.7 1.7 copy.20

commit v3 on v2

--- a/solution.py
+++ b/solution.py
@@ -48,7 +48,7 @@
             barrier, inc=1, device_id={"section": (place + other) % sections}, device_id_type=MESH)
 
     chunk = 16
-    halves = 2 if rows % (2 * chunk) == 0 else 1
+    halves = next(h for h in (4, 2, 1) if rows % (h * chunk) == 0)
     sub = rows // halves
 
     def part(index, h):
@@ -411,9 +411,9 @@
             pltpu.VMEM((experts * rows, tile), jnp.float32),
             pltpu.VMEM((experts * rows, LANES), jnp.float32),
             dma((4,)), dma((experts,)), dma((experts,)),
-            dma((2, 2, chips, 2)), dma((2, chips, 2)), dma((2, chips)), dma((2, chips)),
-            dma((2, chips)), dma((2, chips)), dma((2, chips, 2)), dma((2, 2, chips, 2)),
-            dma((2, 2)), dma((tick_count, 2, 2)), dma((sections,)), dma((tick_count,)), dma(()),
+            dma((2, 2, chips, 4)), dma((2, chips, 4)), dma((2, chips)), dma((2, chips)),
+            dma((2, chips)), dma((2, chips)), dma((2, chips, 4)), dma((2, 2, chips, 4)),
+            dma((2, 4)), dma((tick_count, 2, 4)), dma((sections,)), dma((tick_count,)), dma(()),
         ],
         compiler_params=pltpu.CompilerParams(
             collective_id=0, has_side_effects=True, vmem_limit_bytes=VMEM_LIMIT),

time: 269 us -> 266 us (0.989)
  Pallas kernels: 260 us -> 257 us
    pallas_call x1, Pallas kernels: 260 us -> 257 us  [on_device_relay(): pl.pallas_call(functools.partial(relay_kernel, tick_count, chips, section...]
where the time goes in v3:
time: 266 us; the launch traced here: 265 us
  Pallas kernels  257 us (97%)
  local copies, waits for them, and re-layouts  7.91 us (3%)
    pallas_call x1, Pallas kernels, on_device_relay(): pl.pallas_call(functools.partial(relay_kernel, tick_count, chips, section...  257 us

profile of v3, /device:TPU:0, one launch (start us, length us, event | category | flops | bytes accessed | tf_op | source)
XLA Modules:
  0.0 265.3 jit_solution(15759877357045152002)
XLA Ops:
  0.6 1.3 copy.16
  2.0 0.8 reshape.10
  2.7 0.8 copy.12
  3.5 0.6 pad.9.gates_ref
  4.1 0.1 copy.11
  4.3 0.7 pad.8.ids_ref
  5.0 256.7 %shard_map.77 = (bf16[2,64,2048]{2,1,0:T(8,128)(2,1)}, bf16[4,64,512]{2,1,0:T(8,128)(2,1)}) custom-call(bf16[2,64,2048]{2,1,0:T(8,128)(2,1)} %bitcast.25, f32[2,2048]{1,0:T(2,128)} %bitcast.21, bf16[2,2048,768]{2,1,0:T(8,128)(2,1)} %bitcast.23, bf16[2,768,2048]{2,1,0:T(8,128)(2,1)} %bitcast.24, s32[512,128]{1,0:T(8,128)} %pad.8.ids_ref, f32[64,128]{1,0:T(8,128)} %pad.9.gates_ref), custom_call_target="tpu_custom_call" | custom-call | flops 25769803776 | bytes 12582912 | tf_op jit(solution)/shard_map/pallas_call | solution.py:393
  261.7 1.9 copy.19
  263.6 1.7 copy.20
